TPU v7x, 256 devices: a whole 4x4x8 slice. The times are simulated.
256 devices in a mesh: section: 8 (over x, core), expert: 32 (over z, y).
Axes of the slice: x: 4, y: 4, z: 8, core: 2. Of those that a mesh axis runs over, the one named last changes fastest.
Arguments:
- tokens_fwd: bfloat16 [8, 3072, 4096], P('section', 'expert'), may hold values from -6 to 6
- expert_ids_fwd: int32 [8, 3072, 2], P('section', 'expert'), may hold values from 0 to 15, all different within a row; in each aligned block of 96 rows (0 to 95, 96 to 191, ..., all dimensions but the last counted through in order) at most 16 rows name the same one
- route_weights_fwd: float32 [8, 3072, 2], P('section', 'expert'), may hold values from 0.2 to 1
- tokens_bwd: bfloat16 [8, 3072, 4096], P('section', 'expert'), may hold values from -6 to 6
- cotangent: bfloat16 [8, 3072, 4096], P('section', 'expert'), may hold values from -6 to 6
- expert_ids_bwd: int32 [8, 3072, 2], P('section', 'expert'), may hold values from 0 to 15, all different within a row; in each aligned block of 96 rows (0 to 95, 96 to 191, ..., all dimensions but the last counted through in order) at most 16 rows name the same one
- route_weights_bwd: float32 [8, 3072, 2], P('section', 'expert'), may hold values from 0.2 to 1
- w_gate: bfloat16 [8, 4096, 12288], P('section', None, 'expert'), may hold values from -0.09375 to 0.09375
- w_up: bfloat16 [8, 4096, 12288], P('section', None, 'expert'), may hold values from -0.09375 to 0.09375
- w_down: bfloat16 [8, 12288, 4096], P('section', 'expert'), may hold values from -0.21875 to 0.21875
Outputs:
- next_input: bfloat16 [8, 3072, 4096], P('section', 'expert')
- prev_grad: bfloat16 [8, 3072, 4096], P('section', 'expert')
Inputs may be any that keep to these rules, and one draw needn't show every extreme that they name: `expert_ids_fwd`: each token names 2 different experts. Within the 96 tokens of one index of expert at one section, no expert is named more than 16 times, a bound that some block reaches. `expert_ids_bwd`: as for expert_ids_fwd.
All inputs are finite; a program needn't handle non-finite values.
Results may differ from a plain program's by a relative error of at most 0.0035.
Values may be sent and summed in bfloat16 or wider, within the bound.
A program may use at most 128 MiB of HBM per device.

v0:
```python
import jax
import jax.numpy as jnp
from jax import lax
from jax.sharding import PartitionSpec as P


def passed_along(array, axis, by):
    size = lax.axis_size(axis)
    return lax.ppermute(array, axis, [(i, (i + by) % size) for i in range(size)])


def dispatch_table(expert_ids, dest_count, slot_width, capacity):
    token_count, top_count = expert_ids.shape
    expert_count = dest_count // 2
    flat_ids = expert_ids.reshape(-1)
    onehot = (flat_ids[:, None] == jnp.arange(expert_count, dtype=jnp.int32)[None, :]).astype(
        jnp.int32
    )
    running = jnp.cumsum(onehot, axis=0)
    slot_of = jnp.sum(onehot * running, axis=1) - 1
    slot_keys = flat_ids * capacity + slot_of
    places = jnp.arange(dest_count * slot_width, dtype=jnp.int32)
    device = places // slot_width
    wanted = device // 2 * capacity + places % slot_width
    matches = (wanted[:, None] == slot_keys[None, :]).astype(jnp.bfloat16)
    route_table = jnp.sum(matches.reshape(dest_count * slot_width, token_count, top_count), axis=2)
    return (route_table, slot_keys)


def expert_round(expert_ids, source, stack_count, compute):
    dest_count = lax.axis_size("expert")
    expert_count = dest_count // 2
    token_count, top_count = expert_ids.shape
    capacity = 4 * token_count * top_count // (3 * expert_count)
    feature_width = source.shape[1] // stack_count
    route_table, slot_keys = dispatch_table(expert_ids, dest_count, capacity, capacity)
    outgoing = jnp.dot(route_table, source, preferred_element_type=jnp.float32).astype(jnp.bfloat16)
    outgoing = outgoing.reshape(dest_count, capacity, stack_count, feature_width)
    results = compute(lax.all_to_all(outgoing, "expert", split_axis=0, concat_axis=0, tiled=True))
    returned = lax.all_to_all(results, "expert", split_axis=0, concat_axis=0, tiled=True)
    joined = jnp.sum(returned.reshape(expert_count, 2, capacity, feature_width), axis=1)
    joined = joined.reshape(expert_count * capacity, feature_width)
    return jnp.take(joined, slot_keys, axis=0).reshape(token_count, top_count, feature_width)


def body(
    tokens_fwd,
    expert_ids_fwd,
    route_weights_fwd,
    tokens_bwd,
    cotangent,
    expert_ids_bwd,
    route_weights_bwd,
    w_gate,
    w_up,
    w_down,
):
    gate_local = w_gate[0]
    up_local = w_up[0]
    down_local = w_down[0]
    contract = (((1,), (1,)), ((), ()))

    def forward_rows(row_block):
        item_count, slot_count, stack_count, feature_width = row_block.shape
        flat_in = row_block.reshape(item_count * slot_count, feature_width)
        gate_out = jnp.dot(flat_in, gate_local, preferred_element_type=jnp.float32)
        up_out = jnp.dot(flat_in, up_local, preferred_element_type=jnp.float32)
        hidden = (jax.nn.silu(gate_out) * up_out).astype(jnp.bfloat16)
        expert_out = jnp.dot(hidden, down_local, preferred_element_type=jnp.float32)
        return expert_out.reshape(item_count, slot_count, feature_width)

    def backward_rows(row_block):
        item_count, slot_count, stack_count, feature_width = row_block.shape
        flat_in = row_block[:, :, 0, :].reshape(item_count * slot_count, feature_width)
        flat_cot = row_block[:, :, 1, :].reshape(item_count * slot_count, feature_width)
        gate_out = jnp.dot(flat_in, gate_local, preferred_element_type=jnp.float32)
        up_out = jnp.dot(flat_in, up_local, preferred_element_type=jnp.float32)
        sigmoid_val = jax.nn.sigmoid(gate_out)
        activated = gate_out * sigmoid_val
        act_slope = sigmoid_val * (1.0 + gate_out * (1.0 - sigmoid_val))
        grad_hidden = lax.dot_general(
            flat_cot, down_local, contract, preferred_element_type=jnp.float32
        )
        grad_gate = (grad_hidden * up_out * act_slope).astype(jnp.bfloat16)
        grad_up = (grad_hidden * activated).astype(jnp.bfloat16)
        pulled = lax.dot_general(
            grad_gate, gate_local, contract, preferred_element_type=jnp.float32
        )
        pulled = pulled + lax.dot_general(
            grad_up, up_local, contract, preferred_element_type=jnp.float32
        )
        return pulled.reshape(item_count, slot_count, feature_width)

    inputs_now = tokens_fwd[0]
    picked = expert_round(expert_ids_fwd[0], inputs_now, 1, forward_rows)
    layer_out = inputs_now.astype(jnp.float32) + jnp.sum(
        route_weights_fwd[0][:, :, None] * picked, axis=1
    )
    layer_out = layer_out.astype(jnp.bfloat16)
    next_input = passed_along(layer_out[None], "section", 1)
    stacked = jnp.concatenate([tokens_bwd[0], cotangent[0]], axis=1)
    pulled_rows = expert_round(expert_ids_bwd[0], stacked, 2, backward_rows)
    input_grad = cotangent[0].astype(jnp.float32) + jnp.sum(
        route_weights_bwd[0][:, :, None] * pulled_rows, axis=1
    )
    input_grad = input_grad.astype(jnp.bfloat16)
    prev_grad = passed_along(input_grad[None], "section", -1)
    return (next_input, prev_grad)


def solution(mesh):
    in_specs = (
        P("section", "expert", None),
        P("section", "expert", None),
        P("section", "expert", None),
        P("section", "expert", None),
        P("section", "expert", None),
        P("section", "expert", None),
        P("section", "expert", None),
        P("section", None, "expert"),
        P("section", None, "expert"),
        P("section", "expert", None),
    )
    out_specs = (P("section", "expert", None), P("section", "expert", None))
    return jax.shard_map(body, mesh=mesh, in_specs=in_specs, out_specs=out_specs, check_vma=False)
```

profile of v0, /device:TPU:1, one launch (start us, length us, event | category | flops | bytes accessed | tf_op | source)
XLA Modules:
  0.0 759.9 jit_solution(4956049794479401019)
XLA Ops:
  0.6 0.0 copy-start
  0.7 0.9 copy.42
  1.6 0.1 eq.76
  1.8 0.6 reduce-window.14
  2.3 0.2 slice_reduce_fusion.1
  2.6 0.1 bitcast_bitcast_fusion.1
  2.7 0.1 sub.34
  2.8 0.1 copy.46
  2.9 0.8 copy.49
  3.7 0.1 eq.85
  3.9 0.6 reduce-window.16
  4.5 0.2 slice_reduce_fusion
  4.7 0.1 bitcast_bitcast_fusion
  4.8 0.1 sub.36
  4.9 0.1 copy.53
  5.0 0.2 fusion.45
  5.2 4.3 convolution_convert_fusion.1
  9.5 12.4 %all-to-all-start = ((bf16[32,16,1,4096]{3,1,2,0:T(8,128)(2,1)}), bf16[32,16,1,4096]{3,1,2,0:T(8,128)(2,1)}, u32[]{:S(2)}, u32[]{:S(2)}) async-start(bf16[32,16,1,4096]{3,1,2,0:T(8,128)(2,1)} %bitcast.104), calls=%async_computation | async-start | bytes 8388608 | tf_op jit(solution)/shard_map/all_to_all | solution.py:39
  21.9 7.0 convolution_convert_fusion
  28.9 14.4 %reshape.165 = bf16[32,16,2,4096]{3,2,1,0:T(2,128)(2,1)} reshape(bf16[512,8192]{1,0:T(8,128)(2,1)} %convolution_convert_fusion) | data formatting | bytes 16777216 | tf_op jit(solution)/shard_map/reshape | solution.py:38
  43.3 15.4 %copy.54 = bf16[32,16,2,4096]{3,1,2,0:T(8,128)(2,1)} copy(bf16[32,16,2,4096]{3,2,1,0:T(2,128)(2,1)} %reshape.165) | data formatting | bytes 16777216 | tf_op jit(solution)/shard_map/reshape | solution.py:38
  58.7 56.2 %all-to-all-done = bf16[32,16,1,4096]{3,1,2,0:T(8,128)(2,1)} async-done(((bf16[32,16,1,4096]{3,1,2,0:T(8,128)(2,1)}), bf16[32,16,1,4096]{3,1,2,0:T(8,128)(2,1)}, u32[]{:S(2)}, u32[]{:S(2)}) %all-to-all-start) | async-done | bytes 4194336 | tf_op jit(solution)/shard_map/all_to_all | solution.py:39
  114.9 8.4 %all-to-all-start.2 = ((bf16[32,16,2,4096]{3,1,2,0:T(8,128)(2,1)}), bf16[32,16,2,4096]{3,1,2,0:T(8,128)(2,1)}, u32[]{:S(2)}, u32[]{:S(2)}) async-start(bf16[32,16,2,4096]{3,1,2,0:T(8,128)(2,1)} %copy.54), calls=%async_computation.2 | async-start | bytes 16777216 | tf_op jit(solution)/shard_map/all_to_all | solution.py:39
  123.3 5.5 fusion.13
  128.8 0.0 copy-done
  128.9 0.0 copy-start.3
  128.9 4.7 fusion.32
  133.6 0.0 copy-done.3
  133.6 5.6 fusion
  139.1 172.0 %all-to-all-done.2 = bf16[32,16,2,4096]{3,1,2,0:T(8,128)(2,1)} async-done(((bf16[32,16,2,4096]{3,1,2,0:T(8,128)(2,1)}), bf16[32,16,2,4096]{3,1,2,0:T(8,128)(2,1)}, u32[]{:S(2)}, u32[]{:S(2)}) %all-to-all-start.2) | async-done | bytes 8388640 | tf_op jit(solution)/shard_map/all_to_all | solution.py:39
  311.1 14.2 %all-to-all-start.1 = ((f32[32,16,4096]{2,1,0:T(8,128)}), f32[32,16,4096]{2,1,0:T(8,128)}, u32[]{:S(2)}, u32[]{:S(2)}) async-start(f32[32,16,4096]{2,1,0:T(8,128)} %fusion), calls=%async_computation.1 | async-start | bytes 16777216 | tf_op jit(solution)/shard_map/all_to_all | solution.py:40
  325.3 0.0 copy-start.9
  325.3 4.1 fusion.65
  329.4 0.2 copy-done.9
  329.7 3.2 fusion.11
  332.9 3.2 fusion.2
  336.1 11.4 %fusion.9 = f32[512,4096]{1,0:T(8,128)} fusion(bf16[1,4096,384]{2,1,0:T(8,128)(2,1)} %param.19, f32[512,384]{1,0:T(8,128)} %fusion.2, bf16[512,4096]{1,0:T(8,128)(2,1)} %bitcast.106, bf16[1,4096,384]{2,1,0:T(8,128)(2,1)S(1)} %copy-done, f32[512,384]{1,0:T(8,128)} %fusion.11), kind=kOutput, calls=%fused_computation.16 | convolution fusion | flops 3223191552 | bytes 20447232 | tf_op jit(solution)/shard_map/dot_general | solution.py:86
  347.5 9.5 %convolution_add_fusion = f32[512,4096]{1,0:T(8,128)} fusion(f32[512,4096]{1,0:T(8,128)} %fusion.9, bf16[1,4096,384]{2,1,0:T(8,128)(2,1)S(1)} %copy-done, f32[512,384]{1,0:T(8,128)} %fusion.2, f32[512,384]{1,0:T(8,128)} %fusion.11), kind=kOutput, calls=%fused_computation.5 | convolution fusion | flops 1613889536 | bytes 21495808 | tf_op jit(solution)/shard_map/dot_general | solution.py:89
  357.0 155.9 %all-to-all-done.1 = f32[32,16,4096]{2,1,0:T(8,128)} async-done(((f32[32,16,4096]{2,1,0:T(8,128)}), f32[32,16,4096]{2,1,0:T(8,128)}, u32[]{:S(2)}, u32[]{:S(2)}) %all-to-all-start.1) | async-done | bytes 8388640 | tf_op jit(solution)/shard_map/all_to_all | solution.py:40
  512.9 15.3 %all-to-all-start.3 = ((f32[32,16,4096]{2,1,0:T(8,128)}), f32[32,16,4096]{2,1,0:T(8,128)}, u32[]{:S(2)}, u32[]{:S(2)}) async-start(f32[32,16,4096]{2,1,0:T(8,128)} %bitcast.103), calls=%async_computation.3 | async-start | bytes 16777216 | tf_op jit(solution)/shard_map/all_to_all | solution.py:40
  528.2 0.0 copy-done.7
  528.3 0.1 copy.48
  528.4 0.1 copy.41
  528.5 6.4 bitcast_reduce_fusion.1
  535.0 6.8 gather_fusion
  541.8 2.3 broadcast_select_fusion.1
  544.1 3.3 reshape.162
  547.4 6.7 multiply_reduce_fusion.1
  554.1 1.0 fusion.19
  555.2 2.4 collective-permute-start
  557.6 160.9 %all-to-all-done.3 = f32[32,16,4096]{2,1,0:T(8,128)} async-done(((f32[32,16,4096]{2,1,0:T(8,128)}), f32[32,16,4096]{2,1,0:T(8,128)}, u32[]{:S(2)}, u32[]{:S(2)}) %all-to-all-start.3) | async-done | bytes 8388640 | tf_op jit(solution)/shard_map/all_to_all | solution.py:40
  718.4 6.4 bitcast_reduce_fusion
  724.9 6.8 gather_fusion.1
  731.6 2.3 broadcast_select_fusion
  734.0 3.4 reshape.169
  737.4 0.0 copy-start.6
  737.4 0.0 copy-start.1
  737.4 6.9 multiply_reduce_fusion
  744.3 0.1 fusion.18
  744.5 1.5 collective-permute-start.1
  746.0 0.0 collective-permute-done
  746.0 10.8 %collective-permute-done.1 = bf16[1,96,4096]{2,1,0:T(8,128)(2,1)S(1)} collective-permute-done((bf16[1,96,4096]{2,1,0:T(8,128)(2,1)S(1)}, bf16[1,96,4096]{2,1,0:T(8,128)(2,1)S(1)}, u32[]{:S(2)}, u32[]{:S(2)}) %collective-permute-start.1) | collective-permute-done | bytes 786464 | tf_op jit(solution)/shard_map/ppermute | solution.py:9
  756.7 2.1 copy.69
  758.8 0.9 copy.70
  (30 shorter events, 0.3 us)
Async XLA Ops:
  0.6 128.2 %copy-start = (bf16[1,4096,384]{2,1,0:T(8,128)(2,1)S(1)}, bf16[1,4096,384]{2,1,0:T(8,128)(2,1)}, u32[]{:S(2)}) copy-start(bf16[1,4096,384]{2,1,0:T(8,128)(2,1)} %param.20) | copy-start | bytes 9437188
  9.5 105.4 %all-to-all-start = ((bf16[32,16,1,4096]{3,1,2,0:T(8,128)(2,1)}), bf16[32,16,1,4096]{3,1,2,0:T(8,128)(2,1)}, u32[]{:S(2)}, u32[]{:S(2)}) async-start(bf16[32,16,1,4096]{3,1,2,0:T(8,128)(2,1)} %bitcast.104), calls=%async_computation | async-start | bytes 8388608 | tf_op jit(solution)/shard_map/all_to_all | solution.py:39
  114.9 196.2 %all-to-all-start.2 = ((bf16[32,16,2,4096]{3,1,2,0:T(8,128)(2,1)}), bf16[32,16,2,4096]{3,1,2,0:T(8,128)(2,1)}, u32[]{:S(2)}, u32[]{:S(2)}) async-start(bf16[32,16,2,4096]{3,1,2,0:T(8,128)(2,1)} %copy.54), calls=%async_computation.2 | async-start | bytes 16777216 | tf_op jit(solution)/shard_map/all_to_all | solution.py:39
  128.9 4.7 copy-start.3
  311.1 201.8 %all-to-all-start.1 = ((f32[32,16,4096]{2,1,0:T(8,128)}), f32[32,16,4096]{2,1,0:T(8,128)}, u32[]{:S(2)}, u32[]{:S(2)}) async-start(f32[32,16,4096]{2,1,0:T(8,128)} %fusion), calls=%async_computation.1 | async-start | bytes 16777216 | tf_op jit(solution)/shard_map/all_to_all | solution.py:40
  325.3 4.4 copy-start.9
  329.4 3.4 copy-start.2
  329.7 3.2 copy-start.4
  512.9 15.3 %copy-start.7 = (f32[1,96,2]{1,2,0:T(2,128)S(1)}, f32[1,96,2]{1,2,0:T(2,128)}, u32[]{:S(2)}) copy-start(f32[1,96,2]{1,2,0:T(2,128)} %param.18) | copy-start | bytes 2308
  512.9 15.4 %copy-start.8 = (f32[1,96,2]{1,2,0:T(2,128)S(1)}, f32[1,96,2]{1,2,0:T(2,128)}, u32[]{:S(2)}) copy-start(f32[1,96,2]{1,2,0:T(2,128)} %param.14) | copy-start | bytes 2308
  512.9 205.5 %all-to-all-start.3 = ((f32[32,16,4096]{2,1,0:T(8,128)}), f32[32,16,4096]{2,1,0:T(8,128)}, u32[]{:S(2)}, u32[]{:S(2)}) async-start(f32[32,16,4096]{2,1,0:T(8,128)} %bitcast.103), calls=%async_computation.3 | async-start | bytes 16777216 | tf_op jit(solution)/shard_map/all_to_all | solution.py:40
  547.4 6.7 copy-start.5
  555.2 190.8 %collective-permute-start = (bf16[1,96,4096]{2,1,0:T(8,128)(2,1)}, bf16[1,96,4096]{2,1,0:T(8,128)(2,1)}, u32[]{:S(2)}, u32[]{:S(2)}) collective-permute-start(bf16[1,96,4096]{2,1,0:T(8,128)(2,1)} %fusion.19), channel_id=1, source_target_pairs={{0,32},{32,64},{64,96},{96,128},{128,160},{160,192},{192,224},{224... | collective-permute-start | bytes 2359304 | tf_op jit(solution)/shard_map/ppermute | solution.py:9
  737.4 6.9 copy-start.6
  737.4 22.3 %copy-start.1 = (bf16[1,4096,384]{2,1,0:T(8,128)(2,1)S(1)}, bf16[1,4096,384]{2,1,0:T(8,128)(2,1)}, u32[]{:S(2)}) copy-start(bf16[1,4096,384]{2,1,0:T(8,128)(2,1)} %param.20) | copy-start | bytes 9437188
  744.5 12.2 %collective-permute-start.1 = (bf16[1,96,4096]{2,1,0:T(8,128)(2,1)S(1)}, bf16[1,96,4096]{2,1,0:T(8,128)(2,1)S(1)}, u32[]{:S(2)}, u32[]{:S(2)}) collective-permute-start(bf16[1,96,4096]{2,1,0:T(8,128)(2,1)S(1)} %fusion.18), channel_id=1, source_target_pairs={{0,224},{32,0},{64,32},{96,64},{128,96},{160,128},{192,160},{224,1... | collective-permute-start | bytes 2359304 | tf_op jit(solution)/shard_map/ppermute | solution.py:9
where the time goes:
time: 764 us; the launch traced here: 760 us
  waiting for transfers between devices  556 us (73%)
  local copies, waits for them, and re-layouts  60.4 us (8%)
  matrix products  54.4 us (7%)
  starting transfers between devices  54.1 us (7%)
  other arithmetic  34 us (4%)
    all_to_all x2, waiting for transfers between devices, expert_round(): lax.all_to_all(results, 'expert', split_axis=0, concat_axis=0, tiled=True)  317 us
    all_to_all x2, waiting for transfers between devices, expert_round(): lax.all_to_all(outgoing, 'expert', split_axis=0, concat_axis=0, tiled=True)  228 us
    reshape x2, local copies, waits for them, and re-layouts, expert_round(): outgoing.reshape(dest_count, capacity, stack_count, feature_width)  29.8 us
    all_to_all x2, starting transfers between devices, expert_round(): lax.all_to_all(results, 'expert', split_axis=0, concat_axis=0, tiled=True)  29.5 us
    all_to_all x2, starting transfers between devices, expert_round(): lax.all_to_all(outgoing, 'expert', split_axis=0, concat_axis=0, tiled=True)  20.8 us
  transfers between devices with their start and end apart: 6, of which 5 were waited for; matrix products, arithmetic and copies ran while one was open for 18% of the time, Pallas kernels for 0%

commit v1 on v0

v1 whole, which is shorter than its diff:
```python
import functools

import jax
import jax.numpy as jnp
from jax import lax
from jax.experimental import pallas as pl
from jax.experimental.pallas import tpu as pltpu
from jax.sharding import PartitionSpec as P

MESH = pl.DeviceIdType.MESH
BF16 = jnp.bfloat16
F32 = jnp.float32

WIDTH = 4096
HIDDEN = 384
TOK = 96
CAP = 16
SECTIONS = 8
LONG = 8
SHORT = 4
GROUPS = 4
COLS = 512
STEPS = WIDTH // COLS
NT = (((1,), (1,)), ((), ()))
TN = (((0,), (0,)), ((), ()))

OTHER, OWN, ACROSS, PARTNER, DIAGONAL = range(5)

AT_FORWARD, AT_RECOMPUTE, AT_BACKWARD = 2, 6, 10
AT_SUM = (6, 12)
AT_RETURN = (9, 13)
SLOTS = AT_RETURN[1] + GROUPS


def kernel(
    tok_f,
    tok_b,
    cot,
    meta_f,
    meta_b,
    gate_hbm,
    up_hbm,
    down_hbm,
    out_f,
    out_b,
    source,
    pack,
    rows,
    part_f,
    part_in,
    part_own,
    sums,
    back,
    w_gate,
    w_up,
    w_down,
    factors,
    pick,
    load_sem,
    z_send,
    z_recv,
    own_send,
    own_recv,
    other_send,
    other_recv,
    relay_send,
    relay_recv,
    part_send,
    part_recv,
    sum_send,
    sum_recv,
    back_send,
    back_recv,
    out_send,
    out_recv,
):
    section = lax.axis_index("section")
    expert = lax.axis_index("expert")
    z, y = expert // SHORT, expert % SHORT
    base = expert - y
    pair = y // 2
    partner = {"expert": base + (y + 1 - 2 * (y % 2))}
    across = {"expert": base + (SHORT - 1 - y)}

    def along_z(offset):
        return {"expert": lax.rem(z + offset, LONG) * SHORT + y}

    def along_sections(offset):
        return {"section": lax.rem(section + offset, SECTIONS)}

    loads = [
        pltpu.make_async_copy(tok_f.at[0], source.at[0], load_sem.at[0]),
        pltpu.make_async_copy(tok_b.at[0], source.at[1], load_sem.at[1]),
        pltpu.make_async_copy(cot.at[0], source.at[2], load_sem.at[2]),
        pltpu.make_async_copy(gate_hbm.at[0], w_gate, load_sem.at[3]),
        pltpu.make_async_copy(up_hbm.at[0], w_up, load_sem.at[4]),
        pltpu.make_async_copy(down_hbm.at[0], w_down, load_sem.at[5]),
    ]
    for load in loads:
        load.start()

    barrier = pltpu.get_barrier_semaphore()
    peers = [along_z(offset) for offset in range(1, LONG)]
    peers += [partner, across, along_sections(1), along_sections(SECTIONS - 1)]
    for peer in peers:
        pl.semaphore_signal(barrier, inc=1, device_id=peer, device_id_type=MESH)

    def z_copy(unit, group, side):
        place = 2 * group + side
        offset = group + 1 if side == 0 else LONG - 1 - group
        return pltpu.make_async_remote_copy(
            pack.at[unit, :, place],
            rows.at[unit, pl.ds(OTHER, 2), place],
            z_send.at[unit, place],
            z_recv.at[unit, place],
            device_id=along_z(offset),
            device_id_type=MESH,
        )

    def y_copy(unit, group, plane, to_plane, send, recv, device):
        span = pl.ds(2 * group, 2)
        return pltpu.make_async_remote_copy(
            rows.at[unit, plane, span],
            rows.at[unit, to_plane, span],
            send.at[unit, group],
            recv.at[unit, group],
            device_id=device,
            device_id_type=MESH,
        )

    def own_copy(unit, group):
        return y_copy(unit, group, OWN, PARTNER, own_send, own_recv, partner)

    def other_copy(unit, group):
        return y_copy(unit, group, OTHER, ACROSS, other_send, other_recv, across)

    def relay_copy(unit, group):
        return y_copy(unit, group, ACROSS, DIAGONAL, relay_send, relay_recv, partner)

    def part_copy(batch, group):
        span = pl.ds(2 * group, 2)
        src = part_f.at[:, span] if batch == 0 else pack.at[1, :, span]
        return pltpu.make_async_remote_copy(
            src,
            part_in.at[batch, :, span],
            part_send.at[batch, group],
            part_recv.at[batch, group],
            device_id=partner,
            device_id_type=MESH,
        )

    def sum_copy(batch, group):
        span = pl.ds(2 * group, 2)
        return pltpu.make_async_remote_copy(
            pack.at[2 * batch, 0, span],
            sums.at[batch, OTHER, span],
            sum_send.at[batch, group],
            sum_recv.at[batch, group],
            device_id=across,
            device_id_type=MESH,
        )

    def back_copy(batch, group, side):
        place = 2 * group + side
        offset = LONG - 1 - group if side == 0 else group + 1
        return pltpu.make_async_remote_copy(
            sums.at[batch, :, place],
            back.at[batch, :, place],
            back_send.at[batch, place],
            back_recv.at[batch, place],
            device_id=along_z(offset),
            device_id_type=MESH,
        )

    def out_copy(batch, step):
        cols = pl.ds(pl.multiple_of(step * COLS, COLS), COLS)
        out = out_f if batch == 0 else out_b
        return pltpu.make_async_remote_copy(
            source.at[2 * batch, :, cols],
            out.at[0, :, cols],
            out_send.at[batch, step],
            out_recv.at[batch, step],
            device_id=along_sections(1 if batch == 0 else SECTIONS - 1),
            device_id_type=MESH,
        )

    def both_sides(group, action):
        action(0)
        pl.when(group < GROUPS - 1)(lambda: action(1))

    def route(batch, meta):
        lanes = lax.broadcasted_iota(jnp.int32, (TOK, 128), 1)
        lane_f = lanes.astype(F32)
        first = (meta[:, 0:1] == lane_f).astype(F32)
        second = (meta[:, 1:2] == lane_f).astype(F32)
        earlier = (
            lax.broadcasted_iota(jnp.int32, (TOK, TOK), 0)
            > lax.broadcasted_iota(jnp.int32, (TOK, TOK), 1)
        ).astype(F32)
        rank = jnp.dot(
            earlier.astype(BF16), (first + second).astype(BF16), preferred_element_type=F32
        )
        ahead = (lanes >> 1) - z
        ahead = jnp.where(ahead < 0, ahead + LONG, ahead)
        place = jnp.where(ahead > 4, 2 * (LONG - ahead) - 1, 2 * ahead - 2)
        place = jnp.where(ahead == 0, LONG - 1, place)
        plane = jnp.where((lanes & 1) == pair, OWN, OTHER)
        slots = (plane * (LONG * CAP) + place * CAP).astype(F32) + rank
        wide = lax.broadcasted_iota(jnp.int32, (TOK, 2 * LONG * CAP), 1).astype(F32)
        for k, chosen in enumerate((first, second)):
            slot = jnp.sum(chosen * slots, axis=1, keepdims=True)
            pick[batch, k] = (slot == wide).astype(BF16)

    def pack_rows(unit):
        batch = 0 if unit == 0 else 1
        table = (pick[batch, 0].astype(F32) + pick[batch, 1].astype(F32)).T.astype(BF16)

        def step(i, _):
            cols = pl.ds(pl.multiple_of(i * COLS, COLS), COLS)
            packed = jnp.dot(table, source[unit, :, cols], preferred_element_type=F32)
            packed = packed.astype(BF16).reshape(2, LONG, CAP, COLS)
            pack[unit, :, :, :, cols] = packed
            rows[unit, OTHER : OWN + 1, LONG - 1, :, cols] = packed[:, LONG - 1]
            return 0

        lax.fori_loop(0, STEPS, step, 0)

    loads[0].wait()
    route(0, meta_f)
    pack_rows(0)
    pl.semaphore_wait(barrier, len(peers))
    for group in range(GROUPS):
        for side in range(2 if group < GROUPS - 1 else 1):
            z_copy(0, group, side).start()
    loads[1].wait()
    loads[2].wait()
    route(1, meta_b)
    pack_rows(1)
    pack_rows(2)
    for load in loads[3:]:
        load.wait()

    def expert_rows(unit, group):
        block = rows[unit, OWN : DIAGONAL + 1, pl.ds(2 * group, 2)]
        return block.reshape(4 * 2 * CAP, WIDTH)

    def wait_rows(unit, group):
        own_copy(unit, group).wait_recv()
        relay_copy(unit, group).wait_recv()

    def keep_partial(value, group, part, cols):
        span = pl.ds(2 * group, 2)
        value = value.reshape(2, 2, 2, CAP, COLS)
        part[:, span, :, cols] = value[1].astype(BF16)
        part_own[:, span, :, cols] = value[0]

    def forward(group):
        wait_rows(0, group)
        block = expert_rows(0, group)
        gate = jnp.dot(block, w_gate[...], preferred_element_type=F32)
        up = jnp.dot(block, w_up[...], preferred_element_type=F32)
        hidden = (gate * jax.nn.sigmoid(gate) * up).astype(BF16)

        def step(i, _):
            cols = pl.ds(pl.multiple_of(i * COLS, COLS), COLS)
            value = jnp.dot(hidden, w_down[:, cols], preferred_element_type=F32)
            keep_partial(value, group, part_f, cols)
            return 0

        lax.fori_loop(0, STEPS, step, 0)
        part_copy(0, group).start()

    def recompute(group):
        wait_rows(1, group)
        block = expert_rows(1, group)
        gate = jnp.dot(block, w_gate[...], preferred_element_type=F32)
        up = jnp.dot(block, w_up[...], preferred_element_type=F32)
        q = jax.nn.sigmoid(gate)
        factors[0, group] = up * (q * (1.0 + gate * (1.0 - q)))
        factors[1, group] = gate * q

    def backward(group):
        wait_rows(2, group)
        both_sides(group, lambda side: z_copy(1, group, side).wait_send())
        block = expert_rows(2, group)
        grad = lax.dot_general(block, w_down[...], NT, preferred_element_type=F32)
        grad_gate = (grad * factors[0, group]).astype(BF16)
        grad_up = (grad * factors[1, group]).astype(BF16)

        def step(i, _):
            cols = pl.ds(pl.multiple_of(i * COLS, COLS), COLS)
            value = lax.dot_general(grad_gate, w_gate[cols, :], NT, preferred_element_type=F32)
            value += lax.dot_general(grad_up, w_up[cols, :], NT, preferred_element_type=F32)
            keep_partial(value, group, pack.at[1], cols)
            return 0

        lax.fori_loop(0, STEPS, step, 0)
        part_copy(1, group).start()

    def add_partials(batch, group):
        part_copy(batch, group).wait_recv()
        both_sides(group, lambda side: z_copy(2 * batch, group, side).wait_send())
        span = pl.ds(2 * group, 2)

        def step(i, _):
            cols = pl.ds(pl.multiple_of(i * COLS, COLS), COLS)
            total = part_own[:, span, :, cols] + part_in[batch, :, span, :, cols].astype(F32)
            sums[batch, OWN, span, :, cols] = total[0].astype(BF16)
            pack[2 * batch, 0, span, :, cols] = total[1].astype(BF16)
            return 0

        lax.fori_loop(0, STEPS, step, 0)
        sum_copy(batch, group).start()

    def send_back(batch, group):
        sum_copy(batch, group).wait_recv()
        both_sides(group, lambda side: back_copy(batch, group, side).start())

        @pl.when(group == GROUPS - 1)
        def _():
            back[batch, :, LONG - 1] = sums[batch, :, LONG - 1]

    def slot(t, _):
        def at(first, count, action):
            @pl.when((t >= first) & (t < first + count))
            def _():
                action(t - first)

        def arrivals(item):
            unit, group = item // GROUPS, item % GROUPS
            both_sides(group, lambda side: z_copy(unit, group, side).wait_recv())
            own_copy(unit, group).start()
            other_copy(unit, group).start()

            @pl.when(unit < 2)
            def _():
                both_sides(group, lambda side: z_copy(unit + 1, group, side).start())

        def relay(item):
            unit, group = item // GROUPS, item % GROUPS
            other_copy(unit, group).wait_recv()
            relay_copy(unit, group).start()

        at(0, 3 * GROUPS, arrivals)
        at(1, 3 * GROUPS, relay)
        at(AT_FORWARD, GROUPS, forward)
        at(AT_RECOMPUTE, GROUPS, recompute)
        at(AT_BACKWARD, GROUPS, backward)
        for batch in range(2):
            at(AT_SUM[batch], GROUPS, functools.partial(add_partials, batch))
            at(AT_RETURN[batch], GROUPS, functools.partial(send_back, batch))
        return 0

    lax.fori_loop(0, SLOTS, slot, 0)

    def finish(batch, meta):
        for place in range(LONG - 1):
            back_copy(batch, place // 2, place % 2).wait_recv()

        def step(i, _):
            cols = pl.ds(pl.multiple_of(i * COLS, COLS), COLS)
            returned = back[batch, :, :, :, cols].reshape(2 * LONG * CAP, COLS)
            first = jnp.dot(pick[batch, 0], returned, preferred_element_type=F32)
            second = jnp.dot(pick[batch, 1], returned, preferred_element_type=F32)
            total = meta[:, 2:3] * first + meta[:, 3:4] * second
            total += source[2 * batch, :, cols].astype(F32)
            source[2 * batch, :, cols] = total.astype(BF16)
            out_copy(batch, i).start()
            return 0

        lax.fori_loop(0, STEPS, step, 0)

    finish(0, meta_f)
    finish(1, meta_b)

    def drain(unit, _):
        def of_group(group, _):
            own_copy(unit, group).wait_send()
            other_copy(unit, group).wait_send()
            relay_copy(unit, group).wait_send()
            return 0

        return lax.fori_loop(0, GROUPS, of_group, 0)

    lax.fori_loop(0, 3, drain, 0)
    for batch in range(2):
        for group in range(GROUPS):
            part_copy(batch, group).wait_send()
            sum_copy(batch, group).wait_send()
        for place in range(LONG - 1):
            back_copy(batch, place // 2, place % 2).wait_send()
        for step in range(STEPS):
            out_copy(batch, step).wait()


def body(
    tokens_fwd,
    expert_ids_fwd,
    route_weights_fwd,
    tokens_bwd,
    cotangent,
    expert_ids_bwd,
    route_weights_bwd,
    w_gate,
    w_up,
    w_down,
):
    def meta(expert_ids, route_weights):
        joined = jnp.concatenate([expert_ids[0].astype(F32), route_weights[0]], axis=1)
        return jnp.pad(joined, ((0, 0), (0, 124)))

    anywhere = pl.BlockSpec(memory_space=pl.ANY)
    vmem = pl.BlockSpec(memory_space=pltpu.VMEM)
    out = jax.ShapeDtypeStruct((1, TOK, WIDTH), BF16)
    block = (LONG, CAP, WIDTH)

    def sems(*shape):
        return [pltpu.SemaphoreType.DMA(shape), pltpu.SemaphoreType.DMA(shape)]

    return pl.pallas_call(
        kernel,
        out_shape=(out, out),
        in_specs=[anywhere, anywhere, anywhere, vmem, vmem, anywhere, anywhere, anywhere],
        out_specs=(anywhere, anywhere),
        scratch_shapes=[
            pltpu.VMEM((3, TOK, WIDTH), BF16),
            pltpu.VMEM((3, 2) + block, BF16),
            pltpu.VMEM((3, 5) + block, BF16),
            pltpu.VMEM((2,) + block, BF16),
            pltpu.VMEM((2, 2) + block, BF16),
            pltpu.VMEM((2,) + block, F32),
            pltpu.VMEM((2, 2) + block, BF16),
            pltpu.VMEM((2, 2) + block, BF16),
            pltpu.VMEM((WIDTH, HIDDEN), BF16),
            pltpu.VMEM((WIDTH, HIDDEN), BF16),
            pltpu.VMEM((HIDDEN, WIDTH), BF16),
            pltpu.VMEM((2, GROUPS, 8 * CAP, HIDDEN), F32),
            pltpu.VMEM((2, 2, TOK, 2 * LONG * CAP), BF16),
            pltpu.SemaphoreType.DMA((6,)),
            *sems(3, LONG),
            *sems(3, GROUPS),
            *sems(3, GROUPS),
            *sems(3, GROUPS),
            *sems(2, GROUPS),
            *sems(2, GROUPS),
            *sems(2, LONG),
            *sems(2, STEPS),
        ],
        compiler_params=pltpu.CompilerParams(
            collective_id=0, has_side_effects=True, vmem_limit_bytes=62 * 2**20
        ),
        name="relay_experts",
    )(
        tokens_fwd,
        tokens_bwd,
        cotangent,
        meta(expert_ids_fwd, route_weights_fwd),
        meta(expert_ids_bwd, route_weights_bwd),
        w_gate,
        w_up,
        w_down,
    )


def solution(mesh):
    rows = P("section", "expert", None)
    columns = P("section", None, "expert")
    in_specs = (rows,) * 7 + (columns, columns, rows)
    return jax.shard_map(
        body, mesh=mesh, in_specs=in_specs, out_specs=(rows, rows), check_vma=False
    )
```

time: 764 us -> 303 us (0.40)
  waiting for transfers between devices: 556 us -> 0 us
  Pallas kernels: 0 us -> 294 us
  local copies, waits for them, and re-layouts: 60.4 us -> 5.59 us
  matrix products: 54.4 us -> 0 us
  starting transfers between devices: 54.1 us -> 0 us
  other arithmetic: 34 us -> 2.74 us
    all_to_all x4 -> x0, waiting for transfers between devices: 545 us -> none  [the longest x2 317 us: expert_round(): lax.all_to_all(results, 'expert', split_axis=0, concat_axis=0, tiled=True)]
    pallas_call x0 -> x1, Pallas kernels: none -> 294 us  [body(): pl.pallas_call(kernel, out_shape=(out, out), in_specs=[anywhere, anywhere...]
    dot_general x9 -> x0, matrix products: 54.4 us -> none  [the longest x1 11.4 us: backward_rows(): lax.dot_general(grad_gate, gate_local, contract, preferred_element_type=j...]
    all_to_all x4 -> x0, starting transfers between devices: 50.3 us -> none  [the longest x2 29.5 us: expert_round(): lax.all_to_all(results, 'expert', split_axis=0, concat_axis=0, tiled=True)]
    reshape x4 -> x0, local copies, waits for them, and re-layouts: 36.5 us -> none  [the longest x2 29.8 us: expert_round(): outgoing.reshape(dest_count, capacity, stack_count, feature_width)]
    reduce_sum x7 -> x0, other arithmetic: 26.7 us -> none  [the longest x2 12.9 us: expert_round(): jnp.sum(returned.reshape(expert_count, 2, capacity, feature_width), axis=1)]
    gather x2 -> x0, local copies, waits for them, and re-layouts: 13.6 us -> none  [expert_round(): jnp.take(joined, slot_keys, axis=0)]
    ppermute x2 -> x0, waiting for transfers between devices: 10.8 us -> none  [passed_along(): lax.ppermute(array, axis, [(i, (i + by) % size) for i in range(size)])]
  transfers between devices with their start and end apart: 6 -> 0, of which waited for: 5 -> 0; matrix products, arithmetic and copies ran while one was open for 18% -> 0% of each run, Pallas kernels for 0% -> 0%
where the time goes in v1:
time: 303 us
  Pallas kernels  294 us (97%)
  local copies, waits for them, and re-layouts  5.59 us (2%)
    pallas_call x1, Pallas kernels, body(): pl.pallas_call(kernel, out_shape=(out, out), in_specs=[anywhere, anywhere...  294 us

profile of v1, /device:TPU:1, one launch (start us, length us, event | category | flops | bytes accessed | tf_op | source)
XLA Modules:
  0.0 302.9 jit_solution(6587960238975192976)
XLA Ops:
  0.6 0.7 convert_bitcast_fusion.1
  1.3 0.7 pad_maximum_fusion
  2.0 0.7 convert_bitcast_fusion
  2.7 0.7 pad_maximum_fusion.1
  3.4 0.1 copy.17
  3.5 0.6 pad.8.meta_b
  4.1 0.1 copy.16
  4.2 0.6 pad.7.meta_f
  4.8 294.0 %relay_experts.1 = (bf16[1,96,4096]{2,1,0:T(8,128)(2,1)}, bf16[1,96,4096]{2,1,0:T(8,128)(2,1)}) custom-call(bf16[1,96,4096]{2,1,0:T(8,128)(2,1)} %tok_f.1, bf16[1,96,4096]{2,1,0:T(8,128)(2,1)} %tok_b.1, bf16[1,96,4096]{2,1,0:T(8,128)(2,1)} %cot.1, f32[96,128]{1,0:T(8,128)} %pad.7.meta_f, f32[96,128]{1,0:T(8,128)} %pad.8.meta_b, ...), custom_call_target="tpu_custom_call" | custom-call | tf_op jit(solution)/shard_map/relay_experts/pallas_call | solution.py:420
  298.8 2.1 copy.20
  300.9 2.1 copy.21

commit v2 on v1

v2 whole, which is shorter than its diff:
```python
import jax
import jax.numpy as jnp
from jax import lax
from jax.experimental import pallas as pl
from jax.experimental.pallas import tpu as pltpu
from jax.sharding import PartitionSpec as P

MESH = pl.DeviceIdType.MESH
BF16 = jnp.bfloat16
F32 = jnp.float32

WIDTH = 4096
HIDDEN = 384
TOK = 96
CAP = 16
SECTIONS = 8
LONG = 8
SHORT = 4
GROUPS = 4
COLS = 512
STEPS = WIDTH // COLS
NT = (((1,), (1,)), ((), ()))

OTHER, OWN, ACROSS, PARTNER, DIAGONAL = range(5)

PACK, SEND, ARRIVE, RELAY, FORWARD, RECOMPUTE, BACKWARD, PARTIAL, SUM, BACK, FINISH = range(11)
ORDER = (
    (ARRIVE, 0, 0), (SEND, 0, 1), (SEND, 0, 4), (PACK, 1), (ARRIVE, 1, 0), (PACK, 2),
    (RELAY, 0, 0), (SEND, 0, 5), (SEND, 0, 3), (SEND, 0, 6), (SEND, 0, 2), (SEND, 0, 7),
    (ARRIVE, 2, 0), (RELAY, 1, 0), (ARRIVE, 0, 1), (SEND, 1, 5), (SEND, 1, 6), (RELAY, 2, 0),
    (RELAY, 0, 1), (ARRIVE, 0, 4), (RELAY, 0, 4), (FORWARD, 0), (PARTIAL, 0, 0), (PARTIAL, 0, 1),
    (ARRIVE, 0, 5), (SEND, 2, 5), (SEND, 2, 6), (ARRIVE, 0, 6), (RELAY, 0, 5), (RELAY, 0, 6),
    (SUM, 0, 0), (ARRIVE, 0, 3), (ARRIVE, 0, 2), (BACK, 0, 0), (SUM, 0, 1), (RELAY, 0, 3),
    (SEND, 1, 3), (SEND, 1, 4), (RELAY, 0, 2), (ARRIVE, 0, 7), (BACK, 0, 1), (FORWARD, 2),
    (PARTIAL, 0, 4), (PARTIAL, 0, 5), (RELAY, 0, 7), (SEND, 2, 4), (SEND, 2, 7), (FORWARD, 1),
    (PARTIAL, 0, 3), (PARTIAL, 0, 2), (ARRIVE, 1, 5), (ARRIVE, 1, 6), (RELAY, 1, 5), (SEND, 1, 7),
    (SUM, 0, 4), (RELAY, 1, 6), (BACK, 0, 4), (SUM, 0, 5), (FORWARD, 3), (PARTIAL, 0, 6),
    (PARTIAL, 0, 7), (ARRIVE, 2, 5), (ARRIVE, 2, 6), (SEND, 2, 3), (BACK, 0, 5), (SUM, 0, 3),
    (RELAY, 2, 5), (RELAY, 2, 6), (SUM, 0, 2), (ARRIVE, 1, 4), (ARRIVE, 1, 3), (BACK, 0, 3),
    (BACK, 0, 2), (RELAY, 1, 4), (RELAY, 1, 3), (ARRIVE, 2, 4), (SEND, 1, 2), (RELAY, 2, 4),
    (SUM, 0, 6), (SEND, 2, 2), (BACK, 0, 6), (SUM, 0, 7), (ARRIVE, 2, 7), (BACK, 0, 7),
    (RELAY, 2, 7), (ARRIVE, 1, 7), (RELAY, 1, 7), (ARRIVE, 2, 3), (SEND, 1, 1), (RECOMPUTE, 2),
    (RELAY, 2, 3), (SEND, 2, 1), (BACKWARD, 2), (PARTIAL, 1, 5), (PARTIAL, 1, 4), (ARRIVE, 1, 2),
    (RELAY, 1, 2), (RECOMPUTE, 3), (ARRIVE, 2, 2), (BACKWARD, 3), (PARTIAL, 1, 6), (PARTIAL, 1, 7),
    (RELAY, 2, 2), (SUM, 1, 5), (BACK, 1, 5), (SUM, 1, 4), (BACK, 1, 4), (RECOMPUTE, 1),
    (ARRIVE, 1, 1), (RELAY, 1, 1), (ARRIVE, 2, 1), (FINISH, 0), (SUM, 1, 6), (RELAY, 2, 1),
    (BACK, 1, 6), (SUM, 1, 7), (BACKWARD, 1), (PARTIAL, 1, 3), (PARTIAL, 1, 2), (BACK, 1, 7),
    (RECOMPUTE, 0), (BACKWARD, 0), (PARTIAL, 1, 1), (PARTIAL, 1, 0), (SUM, 1, 3), (BACK, 1, 3),
    (SUM, 1, 2), (BACK, 1, 2), (SUM, 1, 1), (BACK, 1, 1), (SUM, 1, 0), (BACK, 1, 0), (FINISH, 1),
)
ASIDE = 12


def kernel(
    tok_f,
    tok_b,
    cot,
    ids_f,
    ids_b,
    weights_f,
    weights_b,
    gate_hbm,
    up_hbm,
    down_hbm,
    out_f,
    out_b,
    source,
    pack,
    rows,
    part_f,
    part_in,
    part_own,
    sums,
    back,
    w_gate,
    w_up,
    w_down,
    factors,
    residual,
    ids_in_f,
    ids_in_b,
    weights_in_f,
    weights_in_b,
    load_sem,
    z_send,
    z_recv,
    own_send,
    own_recv,
    other_send,
    other_recv,
    relay_send,
    relay_recv,
    part_send,
    part_recv,
    sum_send,
    sum_recv,
    back_send,
    back_recv,
    aside_send,
    aside_recv,
    out_sem,
):
    section = lax.axis_index("section")
    expert = lax.axis_index("expert")
    z, y = expert // SHORT, expert % SHORT
    base = expert - y
    pair = y // 2
    partner = {"expert": base + (y + 1 - 2 * (y % 2))}
    across = {"expert": base + (SHORT - 1 - y)}

    def along_z(offset):
        return {"expert": lax.rem(z + offset, LONG) * SHORT + y}

    def next_section(batch, offset):
        ahead = 1 if batch == 0 else SECTIONS - 1
        return {"section": lax.rem(section + ahead, SECTIONS)} | along_z(offset)

    loads = [
        pltpu.make_async_copy(tok_f.at[0], source.at[0], load_sem.at[0]),
        pltpu.make_async_copy(tok_b.at[0], source.at[1], load_sem.at[1]),
        pltpu.make_async_copy(cot.at[0], source.at[2], load_sem.at[2]),
        pltpu.make_async_copy(gate_hbm.at[0], w_gate, load_sem.at[3]),
        pltpu.make_async_copy(up_hbm.at[0], w_up, load_sem.at[4]),
        pltpu.make_async_copy(down_hbm.at[0], w_down, load_sem.at[5]),
    ]
    for load in loads:
        load.start()

    barrier = pltpu.get_barrier_semaphore()
    peers = [along_z(offset) for offset in range(1, LONG)]
    peers += [partner, across]
    peers += [next_section(batch, offset) for batch in range(2) for offset in range(LONG)]
    for peer in peers:
        pl.semaphore_signal(barrier, inc=1, device_id=peer, device_id_type=MESH)

    def ahead_of(place):
        half = (place + 1) // 2
        return half + (place + 1) % 2 * (LONG - 2 * half)

    def z_copy(unit, place):
        return pltpu.make_async_remote_copy(
            pack.at[unit, :, place],
            rows.at[unit, pl.ds(OTHER, 2), place],
            z_send.at[unit, place],
            z_recv.at[unit, place],
            device_id=along_z(ahead_of(place)),
            device_id_type=MESH,
        )

    def y_copy(unit, place, plane, to_plane, send, recv, device):
        return pltpu.make_async_remote_copy(
            rows.at[unit, plane, place],
            rows.at[unit, to_plane, place],
            send.at[unit, place],
            recv.at[unit, place],
            device_id=device,
            device_id_type=MESH,
        )

    def own_copy(unit, place):
        return y_copy(unit, place, OWN, PARTNER, own_send, own_recv, partner)

    def other_copy(unit, place):
        return y_copy(unit, place, OTHER, ACROSS, other_send, other_recv, across)

    def relay_copy(unit, place):
        return y_copy(unit, place, ACROSS, DIAGONAL, relay_send, relay_recv, partner)

    def part_copy(batch, place):
        return pltpu.make_async_remote_copy(
            part_f.at[:, place] if batch == 0 else pack.at[1, :, place],
            part_in.at[batch, :, place],
            part_send.at[batch, place],
            part_recv.at[batch, place],
            device_id=partner,
            device_id_type=MESH,
        )

    def sum_copy(batch, place):
        return pltpu.make_async_remote_copy(
            pack.at[2 * batch, 0, place],
            sums.at[batch, OTHER, place],
            sum_send.at[batch, place],
            sum_recv.at[batch, place],
            device_id=across,
            device_id_type=MESH,
        )

    def back_copy(batch, place):
        return pltpu.make_async_remote_copy(
            sums.at[batch, :, place],
            back.at[batch, :, place],
            back_send.at[batch, place],
            back_recv.at[batch, place],
            device_id=next_section(batch, LONG - ahead_of(place)),
            device_id_type=MESH,
        )

    def aside_copies(batch):
        pairs = (
            ((tok_f, cot)[batch].at[0], residual.at[batch]),
            ((ids_f, ids_b)[batch], (ids_in_f, ids_in_b)[batch]),
            ((weights_f, weights_b)[batch], (weights_in_f, weights_in_b)[batch]),
        )
        return [
            pltpu.make_async_remote_copy(
                src,
                dst,
                aside_send.at[batch, i],
                aside_recv.at[batch, i],
                device_id=next_section(batch, 0),
                device_id_type=MESH,
            )
            for i, (src, dst) in enumerate(pairs)
        ]

    def out_copy(batch, step):
        cols = pl.ds(pl.multiple_of(step * COLS, COLS), COLS)
        return pltpu.make_async_copy(
            residual.at[batch, :, cols],
            (out_f, out_b)[batch].at[0, :, cols],
            out_sem.at[batch, step],
        )

    def tables(ids):
        names = lax.broadcasted_iota(jnp.int32, (SECTIONS * 2, TOK), 0)
        chosen = [(ids[k : k + 1, :] == names).astype(F32) for k in range(2)]
        earlier = lax.broadcasted_iota(jnp.int32, (TOK, TOK), 0) < lax.broadcasted_iota(
            jnp.int32, (TOK, TOK), 1
        )
        rank = jnp.dot(
            (chosen[0] + chosen[1]).astype(BF16),
            earlier.astype(F32).astype(BF16),
            preferred_element_type=F32,
        )
        ahead = (names >> 1) - z
        ahead = jnp.where(ahead < 0, ahead + LONG, ahead)
        place = jnp.where(ahead > 4, 2 * (LONG - ahead), 2 * ahead - 1)
        place = jnp.where(ahead == 0, 0, place)
        plane = jnp.where((names & 1) == pair, OWN, OTHER)
        slots = (plane * (LONG * CAP) + place * CAP).astype(F32) + rank
        every = lax.broadcasted_iota(jnp.int32, (2 * LONG * CAP, TOK), 0).astype(F32)
        return [
            (jnp.sum(hot * slots, axis=0, keepdims=True) == every).astype(F32) for hot in chosen
        ]

    def pack_rows(unit, table):
        def step(i, _):
            cols = pl.ds(pl.multiple_of(i * COLS, COLS), COLS)
            packed = jnp.dot(table, source[unit, :, cols], preferred_element_type=F32)
            packed = packed.astype(BF16).reshape(2, LONG, CAP, COLS)
            pack[unit, :, :, :, cols] = packed
            rows[unit, OTHER : OWN + 1, 0, :, cols] = packed[:, 0]
            return 0

        lax.fori_loop(0, STEPS, step, 0)

    loads[0].wait()
    pack_rows(0, sum(tables(ids_f)).astype(BF16))
    pl.semaphore_wait(barrier, len(peers))

    def expert_rows(unit, group):
        block = rows[unit, OWN : DIAGONAL + 1, pl.ds(2 * group, 2)]
        return block.reshape(4 * 2 * CAP, WIDTH)

    def pack_unit(unit):
        loads[unit].wait()
        pack_rows(unit, sum(tables(ids_b)).astype(BF16))

    def arrive(unit, place):
        if place > 0:
            z_copy(unit, place).wait_recv()
        own_copy(unit, place).start()
        other_copy(unit, place).start()

    def relay(unit, place):
        other_copy(unit, place).wait_recv()
        relay_copy(unit, place).start()

    def wait_rows(unit, group):
        for place in (2 * group, 2 * group + 1):
            own_copy(unit, place).wait_recv()
            relay_copy(unit, place).wait_recv()

    def keep_partial(value, group, part, cols):
        span = pl.ds(2 * group, 2)
        value = value.reshape(2, 2, 2, CAP, COLS)
        part[:, span, :, cols] = value[1].astype(BF16)
        part_own[:, span, :, cols] = value[0]

    def forward(group):
        wait_rows(0, group)
        block = expert_rows(0, group)
        gate = jnp.dot(block, w_gate[...], preferred_element_type=F32)
        up = jnp.dot(block, w_up[...], preferred_element_type=F32)
        hidden = (gate * jax.nn.sigmoid(gate) * up).astype(BF16)

        def step(i, _):
            cols = pl.ds(pl.multiple_of(i * COLS, COLS), COLS)
            value = jnp.dot(hidden, w_down[:, cols], preferred_element_type=F32)
            keep_partial(value, group, part_f, cols)
            return 0

        lax.fori_loop(0, STEPS, step, 0)

    def recompute(group):
        wait_rows(1, group)
        block = expert_rows(1, group)
        gate = jnp.dot(block, w_gate[...], preferred_element_type=F32)
        up = jnp.dot(block, w_up[...], preferred_element_type=F32)
        q = jax.nn.sigmoid(gate)
        factors[0, group] = up * (q * (1.0 + gate * (1.0 - q)))
        factors[1, group] = gate * q

    def packed_has_left(unit, place):
        if place > 0:
            z_copy(unit, place).wait_send()

    def backward(group):
        wait_rows(2, group)
        packed_has_left(1, 2 * group)
        packed_has_left(1, 2 * group + 1)
        block = expert_rows(2, group)
        grad = lax.dot_general(block, w_down[...], NT, preferred_element_type=F32)
        grad_gate = (grad * factors[0, group]).astype(BF16)
        grad_up = (grad * factors[1, group]).astype(BF16)

        def step(i, _):
            cols = pl.ds(pl.multiple_of(i * COLS, COLS), COLS)
            value = lax.dot_general(grad_gate, w_gate[cols, :], NT, preferred_element_type=F32)
            value += lax.dot_general(grad_up, w_up[cols, :], NT, preferred_element_type=F32)
            keep_partial(value, group, pack.at[1], cols)
            return 0

        lax.fori_loop(0, STEPS, step, 0)

    def add_partials(batch, place):
        part_copy(batch, place).wait_recv()
        packed_has_left(2 * batch, place)

        def step(i, _):
            cols = pl.ds(pl.multiple_of(i * COLS, COLS), COLS)
            total = part_own[:, place, :, cols] + part_in[batch, :, place, :, cols].astype(F32)
            sums[batch, OWN, place, :, cols] = total[0].astype(BF16)
            pack[2 * batch, 0, place, :, cols] = total[1].astype(BF16)
            return 0

        lax.fori_loop(0, STEPS, step, 0)
        sum_copy(batch, place).start()

    def send_back(batch, place):
        sum_copy(batch, place).wait_recv()
        back_copy(batch, place).start()

    def finish(batch):
        for copy in aside_copies(batch):
            copy.wait_recv()
        weights = (weights_in_f, weights_in_b)[batch]
        picks = [hot.T.astype(BF16) for hot in tables((ids_in_f, ids_in_b)[batch])]
        same = lax.broadcasted_iota(jnp.int32, (TOK, TOK), 0) == lax.broadcasted_iota(
            jnp.int32, (TOK, TOK), 1
        )
        scale = [
            jnp.sum(jnp.where(same, weights[k : k + 1, :], 0.0), axis=1, keepdims=True)
            for k in range(2)
        ]
        for place in range(LONG):
            back_copy(batch, place).wait_recv()

        def step(i, _):
            cols = pl.ds(pl.multiple_of(i * COLS, COLS), COLS)
            returned = back[batch, :, :, :, cols].reshape(2 * LONG * CAP, COLS)
            first = jnp.dot(picks[0], returned, preferred_element_type=F32)
            second = jnp.dot(picks[1], returned, preferred_element_type=F32)
            total = scale[0] * first + scale[1] * second
            total += residual[batch, :, cols].astype(F32)
            residual[batch, :, cols] = total.astype(BF16)
            out_copy(batch, i).start()
            return 0

        lax.fori_loop(0, STEPS, step, 0)

    run = {
        PACK: pack_unit,
        SEND: lambda unit, place: z_copy(unit, place).start(),
        ARRIVE: arrive,
        RELAY: relay,
        FORWARD: forward,
        RECOMPUTE: recompute,
        BACKWARD: backward,
        PARTIAL: lambda batch, place: part_copy(batch, place).start(),
        SUM: add_partials,
        BACK: send_back,
        FINISH: finish,
    }
    loaded = False
    for count, (kind, *which) in enumerate(ORDER):
        if kind in (FORWARD, RECOMPUTE) and not loaded:
            for load in loads[3:]:
                load.wait()
            loaded = True
        run[kind](*which)
        if count == ASIDE:
            for batch in range(2):
                for copy in aside_copies(batch):
                    copy.start()

    def drain(unit, _):
        def of_place(place, _):
            own_copy(unit, place).wait_send()
            other_copy(unit, place).wait_send()
            relay_copy(unit, place).wait_send()
            return 0

        return lax.fori_loop(0, LONG, of_place, 0)

    lax.fori_loop(0, 3, drain, 0)
    for batch in range(2):
        for place in range(LONG):
            part_copy(batch, place).wait_send()
            sum_copy(batch, place).wait_send()
            back_copy(batch, place).wait_send()
        for copy in aside_copies(batch):
            copy.wait_send()
        for step in range(STEPS):
            out_copy(batch, step).wait()


def body(
    tokens_fwd,
    expert_ids_fwd,
    route_weights_fwd,
    tokens_bwd,
    cotangent,
    expert_ids_bwd,
    route_weights_bwd,
    w_gate,
    w_up,
    w_down,
):
    anywhere = pl.BlockSpec(memory_space=pl.ANY)
    vmem = pl.BlockSpec(memory_space=pltpu.VMEM)
    out = jax.ShapeDtypeStruct((1, TOK, WIDTH), BF16)
    block = (LONG, CAP, WIDTH)

    def sems(*shape):
        return [pltpu.SemaphoreType.DMA(shape), pltpu.SemaphoreType.DMA(shape)]

    return pl.pallas_call(
        kernel,
        out_shape=(out, out),
        in_specs=[anywhere] * 3 + [vmem] * 4 + [anywhere] * 3,
        out_specs=(anywhere, anywhere),
        scratch_shapes=[
            pltpu.VMEM((3, TOK, WIDTH), BF16),
            pltpu.VMEM((3, 2) + block, BF16),
            pltpu.VMEM((3, 5) + block, BF16),
            pltpu.VMEM((2,) + block, BF16),
            pltpu.VMEM((2, 2) + block, BF16),
            pltpu.VMEM((2,) + block, F32),
            pltpu.VMEM((2, 2) + block, BF16),
            pltpu.VMEM((2, 2) + block, BF16),
            pltpu.VMEM((WIDTH, HIDDEN), BF16),
            pltpu.VMEM((WIDTH, HIDDEN), BF16),
            pltpu.VMEM((HIDDEN, WIDTH), BF16),
            pltpu.VMEM((2, GROUPS, 8 * CAP, HIDDEN), F32),
            pltpu.VMEM((2, TOK, WIDTH), BF16),
            pltpu.VMEM((2, TOK), jnp.int32),
            pltpu.VMEM((2, TOK), jnp.int32),
            pltpu.VMEM((2, TOK), F32),
            pltpu.VMEM((2, TOK), F32),
            pltpu.SemaphoreType.DMA((6,)),
            *sems(3, LONG),
            *sems(3, LONG),
            *sems(3, LONG),
            *sems(3, LONG),
            *sems(2, LONG),
            *sems(2, LONG),
            *sems(2, LONG),
            *sems(2, 3),
            pltpu.SemaphoreType.DMA((2, STEPS)),
        ],
        compiler_params=pltpu.CompilerParams(
            collective_id=0, has_side_effects=True, vmem_limit_bytes=62 * 2**20
        ),
        name="relay_experts",
    )(
        tokens_fwd,
        tokens_bwd,
        cotangent,
        expert_ids_fwd[0].T,
        expert_ids_bwd[0].T,
        route_weights_fwd[0].T,
        route_weights_bwd[0].T,
        w_gate,
        w_up,
        w_down,
    )


def solution(mesh):
    rows = P("section", "expert", None)
    columns = P("section", None, "expert")
    in_specs = (rows,) * 7 + (columns, columns, rows)
    return jax.shard_map(
        body, mesh=mesh, in_specs=in_specs, out_specs=(rows, rows), check_vma=False
    )
```

time: 303 us -> 259 us (0.85)
  Pallas kernels: 294 us -> 254 us
    pallas_call x1, Pallas kernels: 294 us -> 254 us  [body(): pl.pallas_call(kernel, out_shape=(out, out), in_specs=[anywhere] * 3 + [v...]
where the time goes in v2:
time: 259 us
  Pallas kernels  254 us (98%)
  local copies, waits for them, and re-layouts  4.13 us (2%)
    pallas_call x1, Pallas kernels, body(): pl.pallas_call(kernel, out_shape=(out, out), in_specs=[anywhere] * 3 + [v...  254 us

profile of v2, /device:TPU:1, one launch (start us, length us, event | category | flops | bytes accessed | tf_op | source)
XLA Modules:
  0.0 258.7 jit_solution(4614338758608165987)
XLA Ops:
  0.6 254.0 %relay_experts.1 = (bf16[1,96,4096]{2,1,0:T(8,128)(2,1)}, bf16[1,96,4096]{2,1,0:T(8,128)(2,1)}) custom-call(bf16[1,96,4096]{2,1,0:T(8,128)(2,1)} %tok_f.1, bf16[1,96,4096]{2,1,0:T(8,128)(2,1)} %tok_b.1, bf16[1,96,4096]{2,1,0:T(8,128)(2,1)} %cot.1, s32[2,96]{1,0:T(2,128)} %bitcast.12, s32[2,96]{1,0:T(2,128)} %bitcast.13, f32[2,96]{1,0:T(2,128)} %bitcast.14, ...), custom_call_target="tpu_custom_call" | custom-call | tf_op jit(solution)/shard_map/relay_experts/pallas_call | solution.py:449
  254.6 2.1 copy.14
  256.7 2.1 copy.15

commit v3 on v2

--- a/solution.py
+++ b/solution.py
@@ -14,8 +14,11 @@
 TOK = 96
 CAP = 16
 SECTIONS = 8
+EXPERTS = 16
 LONG = 8
 SHORT = 4
+PARTS = 4
+PIECES = LONG + PARTS - 1
 GROUPS = 4
 COLS = 512
 STEPS = WIDTH // COLS
@@ -25,30 +28,39 @@
 
 PACK, SEND, ARRIVE, RELAY, FORWARD, RECOMPUTE, BACKWARD, PARTIAL, SUM, BACK, FINISH = range(11)
 ORDER = (
-    (ARRIVE, 0, 0), (SEND, 0, 1), (SEND, 0, 4), (PACK, 1), (ARRIVE, 1, 0), (PACK, 2),
-    (RELAY, 0, 0), (SEND, 0, 5), (SEND, 0, 3), (SEND, 0, 6), (SEND, 0, 2), (SEND, 0, 7),
-    (ARRIVE, 2, 0), (RELAY, 1, 0), (ARRIVE, 0, 1), (SEND, 1, 5), (SEND, 1, 6), (RELAY, 2, 0),
-    (RELAY, 0, 1), (ARRIVE, 0, 4), (RELAY, 0, 4), (FORWARD, 0), (PARTIAL, 0, 0), (PARTIAL, 0, 1),
-    (ARRIVE, 0, 5), (SEND, 2, 5), (SEND, 2, 6), (ARRIVE, 0, 6), (RELAY, 0, 5), (RELAY, 0, 6),
-    (SUM, 0, 0), (ARRIVE, 0, 3), (ARRIVE, 0, 2), (BACK, 0, 0), (SUM, 0, 1), (RELAY, 0, 3),
-    (SEND, 1, 3), (SEND, 1, 4), (RELAY, 0, 2), (ARRIVE, 0, 7), (BACK, 0, 1), (FORWARD, 2),
-    (PARTIAL, 0, 4), (PARTIAL, 0, 5), (RELAY, 0, 7), (SEND, 2, 4), (SEND, 2, 7), (FORWARD, 1),
-    (PARTIAL, 0, 3), (PARTIAL, 0, 2), (ARRIVE, 1, 5), (ARRIVE, 1, 6), (RELAY, 1, 5), (SEND, 1, 7),
-    (SUM, 0, 4), (RELAY, 1, 6), (BACK, 0, 4), (SUM, 0, 5), (FORWARD, 3), (PARTIAL, 0, 6),
-    (PARTIAL, 0, 7), (ARRIVE, 2, 5), (ARRIVE, 2, 6), (SEND, 2, 3), (BACK, 0, 5), (SUM, 0, 3),
-    (RELAY, 2, 5), (RELAY, 2, 6), (SUM, 0, 2), (ARRIVE, 1, 4), (ARRIVE, 1, 3), (BACK, 0, 3),
-    (BACK, 0, 2), (RELAY, 1, 4), (RELAY, 1, 3), (ARRIVE, 2, 4), (SEND, 1, 2), (RELAY, 2, 4),
-    (SUM, 0, 6), (SEND, 2, 2), (BACK, 0, 6), (SUM, 0, 7), (ARRIVE, 2, 7), (BACK, 0, 7),
-    (RELAY, 2, 7), (ARRIVE, 1, 7), (RELAY, 1, 7), (ARRIVE, 2, 3), (SEND, 1, 1), (RECOMPUTE, 2),
-    (RELAY, 2, 3), (SEND, 2, 1), (BACKWARD, 2), (PARTIAL, 1, 5), (PARTIAL, 1, 4), (ARRIVE, 1, 2),
-    (RELAY, 1, 2), (RECOMPUTE, 3), (ARRIVE, 2, 2), (BACKWARD, 3), (PARTIAL, 1, 6), (PARTIAL, 1, 7),
-    (RELAY, 2, 2), (SUM, 1, 5), (BACK, 1, 5), (SUM, 1, 4), (BACK, 1, 4), (RECOMPUTE, 1),
-    (ARRIVE, 1, 1), (RELAY, 1, 1), (ARRIVE, 2, 1), (FINISH, 0), (SUM, 1, 6), (RELAY, 2, 1),
-    (BACK, 1, 6), (SUM, 1, 7), (BACKWARD, 1), (PARTIAL, 1, 3), (PARTIAL, 1, 2), (BACK, 1, 7),
-    (RECOMPUTE, 0), (BACKWARD, 0), (PARTIAL, 1, 1), (PARTIAL, 1, 0), (SUM, 1, 3), (BACK, 1, 3),
-    (SUM, 1, 2), (BACK, 1, 2), (SUM, 1, 1), (BACK, 1, 1), (SUM, 1, 0), (BACK, 1, 0), (FINISH, 1),
+    (ARRIVE, 0, 0), (SEND, 0, 1), (SEND, 0, 2), (PACK, 1), (ARRIVE, 1, 0), (PACK, 2), (SEND, 0, 6),
+    (SEND, 0, 4), (SEND, 0, 5), (RELAY, 0, 0), (SEND, 0, 3), (SEND, 0, 7), (ARRIVE, 2, 0),
+    (RELAY, 1, 0), (ARRIVE, 0, 1), (ARRIVE, 0, 2), (RELAY, 2, 0), (SEND, 1, 3), (SEND, 2, 4),
+    (RELAY, 0, 1), (RELAY, 0, 2), (SEND, 1, 5), (SEND, 1, 4), (ARRIVE, 0, 5), (ARRIVE, 0, 6),
+    (FORWARD, 0), (PARTIAL, 0, 1), (PARTIAL, 0, 0), (PARTIAL, 0, 8), (PARTIAL, 0, 9),
+    (PARTIAL, 0, 10), (RELAY, 0, 5), (RELAY, 0, 6), (SEND, 2, 6), (ARRIVE, 0, 3), (ARRIVE, 0, 4),
+    (SEND, 1, 7), (SUM, 0, 1), (SUM, 0, 0), (RELAY, 0, 3), (SUM, 0, 8), (SUM, 0, 9), (RELAY, 0, 4),
+    (SUM, 0, 10), (BACK, 0, 1), (ARRIVE, 0, 7), (BACK, 0, 0), (BACK, 0, 8), (BACK, 0, 9),
+    (BACK, 0, 10), (RELAY, 0, 7), (SEND, 2, 5), (ARRIVE, 1, 3), (ARRIVE, 2, 4), (FORWARD, 1),
+    (PARTIAL, 0, 2), (PARTIAL, 0, 3), (SEND, 1, 6), (FORWARD, 2), (PARTIAL, 0, 4), (PARTIAL, 0, 5),
+    (RELAY, 1, 3), (RELAY, 2, 4), (FORWARD, 3), (PARTIAL, 0, 6), (PARTIAL, 0, 7), (ARRIVE, 1, 4),
+    (SEND, 2, 7), (ARRIVE, 1, 5), (RELAY, 1, 4), (SUM, 0, 2), (RELAY, 1, 5), (SEND, 2, 3),
+    (SUM, 0, 3), (BACK, 0, 2), (ARRIVE, 2, 6), (SUM, 0, 4), (BACK, 0, 3), (RELAY, 2, 6),
+    (SEND, 1, 2), (SUM, 0, 5), (BACK, 0, 4), (ARRIVE, 1, 7), (BACK, 0, 5), (RELAY, 1, 7),
+    (SUM, 0, 6), (ARRIVE, 2, 5), (SEND, 2, 2), (SUM, 0, 7), (BACK, 0, 6), (ARRIVE, 1, 6),
+    (RELAY, 2, 5), (BACK, 0, 7), (RELAY, 1, 6), (RECOMPUTE, 2), (ARRIVE, 2, 7), (RELAY, 2, 7),
+    (ARRIVE, 2, 3), (SEND, 1, 1), (RELAY, 2, 3), (ARRIVE, 1, 2), (SEND, 2, 1), (RELAY, 1, 2),
+    (BACKWARD, 2), (RECOMPUTE, 3), (PARTIAL, 1, 4), (PARTIAL, 1, 5), (BACKWARD, 3),
+    (PARTIAL, 1, 6), (PARTIAL, 1, 7), (ARRIVE, 2, 2), (RELAY, 2, 2), (RECOMPUTE, 1), (SUM, 1, 4),
+    (SUM, 1, 5), (BACK, 1, 4), (ARRIVE, 1, 1), (SUM, 1, 6), (BACK, 1, 5), (ARRIVE, 2, 1),
+    (FINISH, 0), (RELAY, 1, 1), (SUM, 1, 7), (BACK, 1, 6), (RELAY, 2, 1), (BACKWARD, 1),
+    (PARTIAL, 1, 3), (PARTIAL, 1, 2), (BACK, 1, 7), (RECOMPUTE, 0), (BACKWARD, 0), (PARTIAL, 1, 1),
+    (PARTIAL, 1, 0), (PARTIAL, 1, 8), (PARTIAL, 1, 9), (PARTIAL, 1, 10), (SUM, 1, 3), (SUM, 1, 2),
+    (BACK, 1, 3), (SUM, 1, 1), (BACK, 1, 2), (SUM, 1, 0), (SUM, 1, 8), (SUM, 1, 9), (SUM, 1, 10),
+    (BACK, 1, 1), (BACK, 1, 0), (BACK, 1, 8), (BACK, 1, 9), (BACK, 1, 10), (FINISH, 1),
 )
 ASIDE = 12
+
+
+def piece_of(piece):
+    if 0 < piece < LONG:
+        return piece, 0, WIDTH
+    return 0, max(piece - LONG + 1, 0) * (WIDTH // PARTS), WIDTH // PARTS
 
 
 def kernel(
@@ -166,32 +178,39 @@
     def relay_copy(unit, place):
         return y_copy(unit, place, ACROSS, DIAGONAL, relay_send, relay_recv, partner)
 
-    def part_copy(batch, place):
+    def part_copy(batch, piece):
+        place, first, width = piece_of(piece)
+        cols = pl.ds(first, width)
+        src = part_f.at[:, place, :, cols] if batch == 0 else pack.at[1, :, place, :, cols]
         return pltpu.make_async_remote_copy(
-            part_f.at[:, place] if batch == 0 else pack.at[1, :, place],
-            part_in.at[batch, :, place],
-            part_send.at[batch, place],
-            part_recv.at[batch, place],
+            src,
+            part_in.at[batch, :, place, :, cols],
+            part_send.at[batch, piece],
+            part_recv.at[batch, piece],
             device_id=partner,
             device_id_type=MESH,
         )
 
-    def sum_copy(batch, place):
+    def sum_copy(batch, piece):
+        place, first, width = piece_of(piece)
+        cols = pl.ds(first, width)
         return pltpu.make_async_remote_copy(
-            pack.at[2 * batch, 0, place],
-            sums.at[batch, OTHER, place],
-            sum_send.at[batch, place],
-            sum_recv.at[batch, place],
+            pack.at[2 * batch, 0, place, :, cols],
+            sums.at[batch, OTHER, place, :, cols],
+            sum_send.at[batch, piece],
+            sum_recv.at[batch, piece],
             device_id=across,
             device_id_type=MESH,
         )
 
-    def back_copy(batch, place):
+    def back_copy(batch, piece):
+        place, first, width = piece_of(piece)
+        cols = pl.ds(first, width)
         return pltpu.make_async_remote_copy(
-            sums.at[batch, :, place],
-            back.at[batch, :, place],
-            back_send.at[batch, place],
-            back_recv.at[batch, place],
+            sums.at[batch, :, place, :, cols],
+            back.at[batch, :, place, :, cols],
+            back_send.at[batch, piece],
+            back_recv.at[batch, piece],
             device_id=next_section(batch, LONG - ahead_of(place)),
             device_id_type=MESH,
         )
@@ -223,7 +242,7 @@
         )
 
     def tables(ids):
-        names = lax.broadcasted_iota(jnp.int32, (SECTIONS * 2, TOK), 0)
+        names = lax.broadcasted_iota(jnp.int32, (EXPERTS, TOK), 0)
         chosen = [(ids[k : k + 1, :] == names).astype(F32) for k in range(2)]
         earlier = lax.broadcasted_iota(jnp.int32, (TOK, TOK), 0) < lax.broadcasted_iota(
             jnp.int32, (TOK, TOK), 1
@@ -334,23 +353,25 @@
 
         lax.fori_loop(0, STEPS, step, 0)
 
-    def add_partials(batch, place):
-        part_copy(batch, place).wait_recv()
-        packed_has_left(2 * batch, place)
+    def add_partials(batch, piece):
+        place, first, width = piece_of(piece)
+        part_copy(batch, piece).wait_recv()
+        if piece < LONG:
+            packed_has_left(2 * batch, place)
 
         def step(i, _):
-            cols = pl.ds(pl.multiple_of(i * COLS, COLS), COLS)
+            cols = pl.ds(pl.multiple_of(first + i * COLS, COLS), COLS)
             total = part_own[:, place, :, cols] + part_in[batch, :, place, :, cols].astype(F32)
             sums[batch, OWN, place, :, cols] = total[0].astype(BF16)
             pack[2 * batch, 0, place, :, cols] = total[1].astype(BF16)
             return 0
 
-        lax.fori_loop(0, STEPS, step, 0)
-        sum_copy(batch, place).start()
-
-    def send_back(batch, place):
-        sum_copy(batch, place).wait_recv()
-        back_copy(batch, place).start()
+        lax.fori_loop(0, width // COLS, step, 0)
+        sum_copy(batch, piece).start()
+
+    def send_back(batch, piece):
+        sum_copy(batch, piece).wait_recv()
+        back_copy(batch, piece).start()
 
     def finish(batch):
         for copy in aside_copies(batch):
@@ -364,8 +385,8 @@
             jnp.sum(jnp.where(same, weights[k : k + 1, :], 0.0), axis=1, keepdims=True)
             for k in range(2)
         ]
-        for place in range(LONG):
-            back_copy(batch, place).wait_recv()
+        for piece in range(PIECES):
+            back_copy(batch, piece).wait_recv()
 
         def step(i, _):
             cols = pl.ds(pl.multiple_of(i * COLS, COLS), COLS)
@@ -388,7 +409,7 @@
         FORWARD: forward,
         RECOMPUTE: recompute,
         BACKWARD: backward,
-        PARTIAL: lambda batch, place: part_copy(batch, place).start(),
+        PARTIAL: lambda batch, piece: part_copy(batch, piece).start(),
         SUM: add_partials,
         BACK: send_back,
         FINISH: finish,
@@ -416,10 +437,10 @@
 
     lax.fori_loop(0, 3, drain, 0)
     for batch in range(2):
-        for place in range(LONG):
-            part_copy(batch, place).wait_send()
-            sum_copy(batch, place).wait_send()
-            back_copy(batch, place).wait_send()
+        for piece in range(PIECES):
+            part_copy(batch, piece).wait_send()
+            sum_copy(batch, piece).wait_send()
+            back_copy(batch, piece).wait_send()
         for copy in aside_copies(batch):
             copy.wait_send()
         for step in range(STEPS):
@@ -474,9 +495,9 @@
             *sems(3, LONG),
             *sems(3, LONG),
             *sems(3, LONG),
-            *sems(2, LONG),
-            *sems(2, LONG),
-            *sems(2, LONG),
+            *sems(2, PIECES),
+            *sems(2, PIECES),
+            *sems(2, PIECES),
             *sems(2, 3),
             pltpu.SemaphoreType.DMA((2, STEPS)),
         ],

time: 259 us -> 257 us (level)
  no operation moved by 1% of the time
where the time goes in v3:
time: 257 us
  Pallas kernels  252 us (98%)
  local copies, waits for them, and re-layouts  4.13 us (2%)
    pallas_call x1, Pallas kernels, body(): pl.pallas_call(kernel, out_shape=(out, out), in_specs=[anywhere] * 3 + [v...  252 us

profile of v3, /device:TPU:1, one launch (start us, length us, event | category | flops | bytes accessed | tf_op | source)
XLA Modules:
  0.0 257.0 jit_solution(12243324129245859800)
XLA Ops:
  0.6 252.2 %relay_experts.1 = (bf16[1,96,4096]{2,1,0:T(8,128)(2,1)}, bf16[1,96,4096]{2,1,0:T(8,128)(2,1)}) custom-call(bf16[1,96,4096]{2,1,0:T(8,128)(2,1)} %tok_f.1, bf16[1,96,4096]{2,1,0:T(8,128)(2,1)} %tok_b.1, bf16[1,96,4096]{2,1,0:T(8,128)(2,1)} %cot.1, s32[2,96]{1,0:T(2,128)} %bitcast.12, s32[2,96]{1,0:T(2,128)} %bitcast.13, f32[2,96]{1,0:T(2,128)} %bitcast.14, ...), custom_call_target="tpu_custom_call" | custom-call | tf_op jit(solution)/shard_map/relay_experts/pallas_call | solution.py:470
  252.9 2.1 copy.14
  254.9 2.1 copy.15

commit v4 on v3

--- a/solution.py
+++ b/solution.py
@@ -28,28 +28,28 @@
 
 PACK, SEND, ARRIVE, RELAY, FORWARD, RECOMPUTE, BACKWARD, PARTIAL, SUM, BACK, FINISH = range(11)
 ORDER = (
-    (ARRIVE, 0, 0), (SEND, 0, 1), (SEND, 0, 2), (PACK, 1), (ARRIVE, 1, 0), (PACK, 2), (SEND, 0, 6),
-    (SEND, 0, 4), (SEND, 0, 5), (RELAY, 0, 0), (SEND, 0, 3), (SEND, 0, 7), (ARRIVE, 2, 0),
-    (RELAY, 1, 0), (ARRIVE, 0, 1), (ARRIVE, 0, 2), (RELAY, 2, 0), (SEND, 1, 3), (SEND, 2, 4),
-    (RELAY, 0, 1), (RELAY, 0, 2), (SEND, 1, 5), (SEND, 1, 4), (ARRIVE, 0, 5), (ARRIVE, 0, 6),
-    (FORWARD, 0), (PARTIAL, 0, 1), (PARTIAL, 0, 0), (PARTIAL, 0, 8), (PARTIAL, 0, 9),
-    (PARTIAL, 0, 10), (RELAY, 0, 5), (RELAY, 0, 6), (SEND, 2, 6), (ARRIVE, 0, 3), (ARRIVE, 0, 4),
-    (SEND, 1, 7), (SUM, 0, 1), (SUM, 0, 0), (RELAY, 0, 3), (SUM, 0, 8), (SUM, 0, 9), (RELAY, 0, 4),
-    (SUM, 0, 10), (BACK, 0, 1), (ARRIVE, 0, 7), (BACK, 0, 0), (BACK, 0, 8), (BACK, 0, 9),
-    (BACK, 0, 10), (RELAY, 0, 7), (SEND, 2, 5), (ARRIVE, 1, 3), (ARRIVE, 2, 4), (FORWARD, 1),
-    (PARTIAL, 0, 2), (PARTIAL, 0, 3), (SEND, 1, 6), (FORWARD, 2), (PARTIAL, 0, 4), (PARTIAL, 0, 5),
-    (RELAY, 1, 3), (RELAY, 2, 4), (FORWARD, 3), (PARTIAL, 0, 6), (PARTIAL, 0, 7), (ARRIVE, 1, 4),
-    (SEND, 2, 7), (ARRIVE, 1, 5), (RELAY, 1, 4), (SUM, 0, 2), (RELAY, 1, 5), (SEND, 2, 3),
-    (SUM, 0, 3), (BACK, 0, 2), (ARRIVE, 2, 6), (SUM, 0, 4), (BACK, 0, 3), (RELAY, 2, 6),
-    (SEND, 1, 2), (SUM, 0, 5), (BACK, 0, 4), (ARRIVE, 1, 7), (BACK, 0, 5), (RELAY, 1, 7),
-    (SUM, 0, 6), (ARRIVE, 2, 5), (SEND, 2, 2), (SUM, 0, 7), (BACK, 0, 6), (ARRIVE, 1, 6),
-    (RELAY, 2, 5), (BACK, 0, 7), (RELAY, 1, 6), (RECOMPUTE, 2), (ARRIVE, 2, 7), (RELAY, 2, 7),
-    (ARRIVE, 2, 3), (SEND, 1, 1), (RELAY, 2, 3), (ARRIVE, 1, 2), (SEND, 2, 1), (RELAY, 1, 2),
-    (BACKWARD, 2), (RECOMPUTE, 3), (PARTIAL, 1, 4), (PARTIAL, 1, 5), (BACKWARD, 3),
-    (PARTIAL, 1, 6), (PARTIAL, 1, 7), (ARRIVE, 2, 2), (RELAY, 2, 2), (RECOMPUTE, 1), (SUM, 1, 4),
-    (SUM, 1, 5), (BACK, 1, 4), (ARRIVE, 1, 1), (SUM, 1, 6), (BACK, 1, 5), (ARRIVE, 2, 1),
-    (FINISH, 0), (RELAY, 1, 1), (SUM, 1, 7), (BACK, 1, 6), (RELAY, 2, 1), (BACKWARD, 1),
-    (PARTIAL, 1, 3), (PARTIAL, 1, 2), (BACK, 1, 7), (RECOMPUTE, 0), (BACKWARD, 0), (PARTIAL, 1, 1),
+    (ARRIVE, 0, 0), (SEND, 0, 2), (SEND, 0, 1), (PACK, 1), (ARRIVE, 1, 0), (PACK, 2),
+    (ARRIVE, 2, 0), (SEND, 0, 4), (RELAY, 0, 0), (SEND, 0, 5), (SEND, 0, 6), (SEND, 0, 3),
+    (SEND, 0, 7), (RELAY, 1, 0), (SEND, 1, 4), (SEND, 1, 5), (ARRIVE, 0, 2), (ARRIVE, 0, 1),
+    (RELAY, 2, 0), (RELAY, 0, 2), (RELAY, 0, 1), (SEND, 2, 4), (ARRIVE, 0, 4), (SEND, 1, 3),
+    (RELAY, 0, 4), (ARRIVE, 0, 5), (FORWARD, 0), (PARTIAL, 0, 1), (PARTIAL, 0, 0), (PARTIAL, 0, 8),
+    (PARTIAL, 0, 9), (PARTIAL, 0, 10), (RELAY, 0, 5), (SEND, 1, 6), (SEND, 2, 5), (ARRIVE, 0, 6),
+    (ARRIVE, 0, 3), (RELAY, 0, 6), (SUM, 0, 1), (SUM, 0, 0), (RELAY, 0, 3), (SUM, 0, 8),
+    (SUM, 0, 9), (SEND, 2, 6), (ARRIVE, 0, 7), (SUM, 0, 10), (BACK, 0, 1), (BACK, 0, 0),
+    (BACK, 0, 8), (BACK, 0, 9), (FORWARD, 2), (PARTIAL, 0, 4), (PARTIAL, 0, 5), (RELAY, 0, 7),
+    (BACK, 0, 10), (SEND, 1, 7), (ARRIVE, 1, 4), (FORWARD, 1), (PARTIAL, 0, 2), (PARTIAL, 0, 3),
+    (ARRIVE, 1, 5), (RELAY, 1, 4), (SEND, 2, 7), (ARRIVE, 2, 4), (RELAY, 1, 5), (SUM, 0, 4),
+    (RELAY, 2, 4), (ARRIVE, 1, 3), (SUM, 0, 5), (BACK, 0, 4), (FORWARD, 3), (PARTIAL, 0, 6),
+    (PARTIAL, 0, 7), (SEND, 2, 3), (RELAY, 1, 3), (BACK, 0, 5), (ARRIVE, 1, 6), (SUM, 0, 2),
+    (RELAY, 1, 6), (ARRIVE, 2, 5), (SUM, 0, 3), (BACK, 0, 2), (RELAY, 2, 5), (BACK, 0, 3),
+    (SEND, 1, 2), (ARRIVE, 2, 6), (RECOMPUTE, 2), (SEND, 2, 2), (RELAY, 2, 6), (ARRIVE, 1, 7),
+    (SUM, 0, 6), (SEND, 1, 1), (RELAY, 1, 7), (SUM, 0, 7), (BACK, 0, 6), (SEND, 2, 1),
+    (ARRIVE, 2, 7), (BACK, 0, 7), (RELAY, 2, 7), (ARRIVE, 2, 3), (BACKWARD, 2), (PARTIAL, 1, 4),
+    (PARTIAL, 1, 5), (RELAY, 2, 3), (RECOMPUTE, 3), (ARRIVE, 1, 2), (BACKWARD, 3), (ARRIVE, 2, 2),
+    (PARTIAL, 1, 7), (PARTIAL, 1, 6), (RELAY, 1, 2), (SUM, 1, 4), (RELAY, 2, 2), (ARRIVE, 1, 1),
+    (SUM, 1, 5), (BACK, 1, 4), (RELAY, 1, 1), (ARRIVE, 2, 1), (BACK, 1, 5), (RELAY, 2, 1),
+    (SUM, 1, 7), (FINISH, 0), (SUM, 1, 6), (BACK, 1, 7), (RECOMPUTE, 1), (BACKWARD, 1),
+    (PARTIAL, 1, 3), (PARTIAL, 1, 2), (BACK, 1, 6), (RECOMPUTE, 0), (BACKWARD, 0), (PARTIAL, 1, 1),
     (PARTIAL, 1, 0), (PARTIAL, 1, 8), (PARTIAL, 1, 9), (PARTIAL, 1, 10), (SUM, 1, 3), (SUM, 1, 2),
     (BACK, 1, 3), (SUM, 1, 1), (BACK, 1, 2), (SUM, 1, 0), (SUM, 1, 8), (SUM, 1, 9), (SUM, 1, 10),
     (BACK, 1, 1), (BACK, 1, 0), (BACK, 1, 8), (BACK, 1, 9), (BACK, 1, 10), (FINISH, 1),

time: 257 us -> 257 us (level)
  no operation moved by 1% of the time
where the time goes in v4:
time: 257 us
  Pallas kernels  252 us (98%)
  local copies, waits for them, and re-layouts  4.13 us (2%)
    pallas_call x1, Pallas kernels, body(): pl.pallas_call(kernel, out_shape=(out, out), in_specs=[anywhere] * 3 + [v...  252 us

profile of v4, /device:TPU:1, one launch (start us, length us, event | category | flops | bytes accessed | tf_op | source)
XLA Modules:
  0.0 256.9 jit_solution(4685248440597986060)
XLA Ops:
  0.6 252.1 %relay_experts.1 = (bf16[1,96,4096]{2,1,0:T(8,128)(2,1)}, bf16[1,96,4096]{2,1,0:T(8,128)(2,1)}) custom-call(bf16[1,96,4096]{2,1,0:T(8,128)(2,1)} %tok_f.1, bf16[1,96,4096]{2,1,0:T(8,128)(2,1)} %tok_b.1, bf16[1,96,4096]{2,1,0:T(8,128)(2,1)} %cot.1, s32[2,96]{1,0:T(2,128)} %bitcast.12, s32[2,96]{1,0:T(2,128)} %bitcast.13, f32[2,96]{1,0:T(2,128)} %bitcast.14, ...), custom_call_target="tpu_custom_call" | custom-call | tf_op jit(solution)/shard_map/relay_experts/pallas_call | solution.py:470
  252.8 2.1 copy.14
  254.8 2.1 copy.15
